TPU v7x, 128 devices: a whole 4x4x4 slice. The times are simulated.
128 devices in a mesh: row: 8 (over x, core), col: 16 (over y, z).
Axes of the slice: x: 4, y: 4, z: 4, core: 2. Of those that a mesh axis runs over, the one named last changes fastest.
Arguments:
- amplitudes: float32 [256, 32768], P(('row', 'col')), may hold values from -6 to 6
- integrals: float32 [16384, 32768], P('row', 'col'), may hold values from -0.09375 to 0.09375
- ij_irrep: int32 [256], replicated, may hold values from 0 to 7
- ab_irrep: int32 [16384], P('row'), may hold values from 0 to 7
- cd_irrep: int32 [32768], P('col'), may hold values from 0 to 7
Outputs:
- ladder_out: float32 [256, 16384], P(('row', 'col'))
All inputs are finite; a program needn't handle non-finite values.
Results may differ from a plain program's by a relative error of at most 0.000078.
Values sent between devices are 32-bit elements; how exact they have to be, the bound alone decides.
A program may use at most 64 MiB of HBM per device.

v0:
```python
import jax
import jax.numpy as jnp
from jax import lax
from jax.sharding import PartitionSpec as P


def contract(amp_block, integrals):
    return lax.dot_general(
        amp_block,
        integrals,
        (((1,), (1,)), ((), ())),
        precision=lax.Precision.HIGHEST,
        preferred_element_type=jnp.float32,
    )


def body(amplitudes, integrals, ij_irrep, ab_irrep, cd_irrep):
    by_column = lax.all_to_all(amplitudes, "col", split_axis=1, concat_axis=0, tiled=True)
    gathered = lax.all_gather(by_column, "row", axis=0, tiled=True)
    row_count = lax.axis_size("row")
    col_count = lax.axis_size("col")
    pair_count = gathered.shape[0]
    col_width = gathered.shape[1]
    own_pairs = pair_count // (row_count * col_count)
    ordered = (
        gathered.reshape(row_count, col_count, own_pairs, col_width)
        .transpose(1, 0, 2, 3)
        .reshape(pair_count, col_width)
    )
    pair_irrep = (
        ij_irrep.reshape(row_count, col_count, own_pairs).transpose(1, 0, 2).reshape(pair_count)
    )
    masked = jnp.where(cd_irrep[None, :] == pair_irrep[:, None], ordered, 0.0)
    product = contract(masked, integrals)
    shared = lax.psum_scatter(
        jnp.where(pair_irrep[:, None] == ab_irrep[None, :], product, 0.0),
        "col",
        scatter_dimension=0,
        tiled=True,
    )
    owned = lax.all_to_all(shared, "row", split_axis=0, concat_axis=1, tiled=True)
    return owned


def solution(mesh):
    in_specs = (P(("row", "col"), None), P("row", "col"), P(), P("row"), P("col"))
    out_specs = P(("row", "col"), None)
    return jax.shard_map(body, mesh=mesh, in_specs=in_specs, out_specs=out_specs, check_vma=False)
```

profile of v0, /device:TPU:1, one launch (start us, length us, event | category | flops | bytes accessed | tf_op | source)
XLA Modules:
  0.0 166.6 jit_solution(9258753089181089107)
XLA Ops:
  6.5 0.0 all-gather.2.cloned.1.call-start
  6.5 16.1 %all_to_all.38 = f32[2,16,2048]{2,0,1:T(2,128)S(1)} all-to-all(f32[2,16,2048]{2,0,1:T(2,128)} %bitcast.11), channel_id=1, replica_groups=mesh['row'=8,'col'=16] {'col'}, dimensions={1} | all-to-all | bytes 524288 | tf_op jit(solution)/shard_map/all_to_all | solution.py:18
  22.6 0.9 all_to_all.31
  23.5 0.0 all-gather.2.cloned.1.call-update
  23.5 0.0 reduce-scatter.2.cloned.1.call-start
  23.6 0.8 reshape.18
  24.4 0.1 eq.12
  24.5 24.0 %all-gather.2.cloned.1.call-done = f32[256,2048]{1,0:T(8,128)} async-done(((f32[32,2048]{1,0:T(8,128)}), f32[256,2048]{1,0:T(8,128)}) %all-gather.2.cloned.1.call-update) | async-done | bytes 2097168 | tf_op jit(solution)/shard_map/all_gather | solution.py:19
  48.5 2.5 %reshape.19 = f32[8,16,2,2048]{3,2,1,0:T(2,128)S(1)} reshape(f32[256,2048]{1,0:T(8,128)} %all-gather.2.cloned.1.call-done) | data formatting | bytes 4194304 | tf_op jit(solution)/shard_map/reshape | solution.py:26
  51.0 1.6 copy.9
  52.6 0.0 copy-start
  52.6 0.0 copy-start.1
  52.6 2.7 %reshape.20 = f32[256,2048]{1,0:T(8,128)S(1)} reshape(f32[16,8,2,2048]{3,2,1,0:T(2,128)} %copy.9) | data formatting | bytes 4194304 | tf_op jit(solution)/shard_map/reshape | solution.py:28
  55.3 0.0 copy-done
  55.3 0.0 copy-done.1
  55.3 18.1 %convolution_select_fusion = f32[256,2048]{1,0:T(8,128)} fusion(f32[2048,2048]{1,0:T(8,128)} %param.6, f32[256,2048]{1,0:T(8,128)S(1)} %reshape.20, s32[2048]{0:T(1024)S(1)} %copy-done, s32[2048]{0:T(1024)S(1)} %copy-done.1, s32[256]{0:T(256)S(1)} %eq.12), kind=kOutput, calls=%fused_computation | convolution fusion | flops 12886999040 | bytes 20988928 | tf_op jit(solution)/shard_map/dot_general | solution.py:8
  73.5 0.0 reduce-scatter.2.cloned.1.call-update
  73.5 73.0 %reduce-scatter.2.cloned.1.call-done = f32[16,2048]{1,0:T(8,128)} async-done(((f32[256,2048]{1,0:T(8,128)}), f32[16,2048]{1,0:T(8,128)}) %reduce-scatter.2.cloned.1.call-update) | async-done | bytes 131088 | tf_op jit(solution)/shard_map/reduce_scatter | solution.py:35
  146.5 1.0 all_to_all.32
  147.5 11.6 %all_to_all.39 = f32[8,2,2048]{2,1,0:T(2,128)S(1)} all-to-all(f32[8,2,2048]{2,1,0:T(2,128)S(1)} %all_to_all.32), channel_id=1, replica_groups=mesh['row'=8,'col'=16] {'row'}, dimensions={0} | all-to-all | bytes 262144 | tf_op jit(solution)/shard_map/all_to_all | solution.py:41
  159.1 0.7 copy.12
  (1 shorter events, 0.0 us)
Async XLA Ops:
  6.5 42.0 %all-gather.2.cloned.1.call-start = ((), (), s32[]{:S(2)}) async-start(), calls=%async_computation.3 | async-start | bytes 2359296 | tf_op jit(solution)/shard_map/all_gather | solution.py:19
  23.5 123.0 %reduce-scatter.2.cloned.1.call-start = ((), (), s32[]{:S(2)}) async-start(), calls=%async_computation.4 | async-start | bytes 2228224 | tf_op jit(solution)/shard_map/reduce_scatter | solution.py:35
  52.6 2.7 %copy-start = (s32[2048]{0:T(1024)S(1)}, s32[2048]{0:T(1024)}, u32[]{:S(2)}) copy-start(s32[2048]{0:T(1024)} %param.9) | copy-start | bytes 24580
  52.6 2.7 %copy-start.1 = (s32[2048]{0:T(1024)S(1)}, s32[2048]{0:T(1024)}, u32[]{:S(2)}) copy-start(s32[2048]{0:T(1024)} %param.8) | copy-start | bytes 24580
Sparse Core Ops, SparseCore 0:
  23.6 24.8 all-gather.1
  73.6 72.8 reduce-scatter.1
where the time goes:
time: 167 us
  waiting for transfers between devices  97 us (58%)
  blocking collectives  27.6 us (17%)
  matrix products  18.1 us (11%)
  between operations  13.5 us (8%)
  local copies, waits for them, and re-layouts  10.3 us (6%)
    reduce_scatter x1, waiting for transfers between devices, body(): lax.psum_scatter(jnp.where(pair_irrep[:, None] == ab_irrep[None, :], prod...  73 us
    all_gather x1, waiting for transfers between devices, body(): gathered = lax.all_gather(by_column, 'row', axis=0, tiled=True)  24 us
    dot_general x1, matrix products, contract(): lax.dot_general(amp_block, integrals, (((1,), (1,)), ((), ())), precision...  18.1 us
    all_to_all x1, blocking collectives, body(): lax.all_to_all(amplitudes, 'col', split_axis=1, concat_axis=0, tiled=True)  16.1 us
    all_to_all x1, blocking collectives, body(): lax.all_to_all(shared, 'row', split_axis=0, concat_axis=1, tiled=True)  11.6 us
  transfers between devices with their start and end apart: 2, of which 2 were waited for; matrix products, arithmetic and copies ran while one was open for 1% of the time, Pallas kernels for 0%

commit v1 on v0

--- a/solution.py
+++ b/solution.py
@@ -16,7 +16,9 @@
 
 def body(amplitudes, integrals, ij_irrep, ab_irrep, cd_irrep):
     by_column = lax.all_to_all(amplitudes, "col", split_axis=1, concat_axis=0, tiled=True)
-    gathered = lax.all_gather(by_column, "row", axis=0, tiled=True)
+    gathered = jnp.concatenate(
+        lax.all_to_all(jnp.stack([by_column] * lax.axis_size("row")), "row", 0, 0), axis=0
+    )
     row_count = lax.axis_size("row")
     col_count = lax.axis_size("col")
     pair_count = gathered.shape[0]

time: 167 us -> 172 us (1.030)
  starting transfers between devices: 0.04 us -> 6.44 us
    all_to_all x0 -> x1, waiting for transfers between devices: none -> 26 us  [body(): lax.all_to_all(jnp.stack([by_column] * lax.axis_size('row')), 'row', 0, 0)]
    all_gather x1 -> x0, waiting for transfers between devices: 24 us -> none  [body(): gathered = lax.all_gather(by_column, 'row', axis=0, tiled=True)]
    all_to_all x0 -> x1, starting transfers between devices: none -> 6.44 us  [body(): lax.all_to_all(jnp.stack([by_column] * lax.axis_size('row')), 'row', 0, 0)]
    reduce_scatter x1, waiting for transfers between devices: 73 us -> 69.4 us  [body(): lax.psum_scatter(jnp.where(pair_irrep[:, None] == ab_irrep[None, :], prod...]
    reshape x1 -> x0, local copies, waits for them, and re-layouts: 2.49 us -> none  [body(): gathered.reshape(row_count, col_count, own_pairs, col_width)]
    another operation x0 -> x2, local copies, waits for them, and re-layouts: none -> 1.76 us  [body(): jnp.stack([by_column] * lax.axis_size('row'))]
  transfers between devices with their start and end apart: 2 -> 2, of which waited for: 2 -> 2; matrix products, arithmetic and copies ran while one was open for 1% -> 0% of each run, Pallas kernels for 0% -> 0%
where the time goes in v1:
time: 172 us
  waiting for transfers between devices  95.5 us (56%)
  blocking collectives  27.7 us (16%)
  matrix products  18.1 us (11%)
  between operations  13.4 us (8%)
  local copies, waits for them, and re-layouts  10.6 us (6%)
  starting transfers between devices  6.44 us (4%)
    reduce_scatter x1, waiting for transfers between devices, body(): lax.psum_scatter(jnp.where(pair_irrep[:, None] == ab_irrep[None, :], prod...  69.4 us
    all_to_all x1, waiting for transfers between devices, body(): lax.all_to_all(jnp.stack([by_column] * lax.axis_size('row')), 'row', 0, 0)  26 us
    dot_general x1, matrix products, contract(): lax.dot_general(amp_block, integrals, (((1,), (1,)), ((), ())), precision...  18.1 us
    all_to_all x1, blocking collectives, body(): lax.all_to_all(amplitudes, 'col', split_axis=1, concat_axis=0, tiled=True)  16.1 us
    all_to_all x1, blocking collectives, body(): lax.all_to_all(shared, 'row', split_axis=0, concat_axis=1, tiled=True)  11.6 us
    all_to_all x1, starting transfers between devices, body(): lax.all_to_all(jnp.stack([by_column] * lax.axis_size('row')), 'row', 0, 0)  6.44 us
  transfers between devices with their start and end apart: 2, of which 2 were waited for; matrix products, arithmetic and copies ran while one was open for 0% of the time, Pallas kernels for 0%

profile of v1, /device:TPU:1, one launch (start us, length us, event | category | flops | bytes accessed | tf_op | source)
XLA Modules:
  0.0 171.8 jit_solution(13993831416329387181)
XLA Ops:
  6.5 16.1 %all_to_all.40 = f32[2,16,2048]{2,0,1:T(2,128)S(1)} all-to-all(f32[2,16,2048]{2,0,1:T(2,128)} %bitcast.13), channel_id=1, replica_groups=mesh['row'=8,'col'=16] {'col'}, dimensions={1} | all-to-all | bytes 524288 | tf_op jit(solution)/shard_map/all_to_all | solution.py:18
  22.6 0.2 stack.4
  22.8 1.6 stack.5
  24.4 0.0 copy-start.2
  24.4 6.4 %all-to-all-start.1 = ((f32[8,32,2048]{2,1,0:T(8,128)}), f32[8,32,2048]{2,1,0:T(8,128)S(1)}, u32[]{:S(2)}, u32[]{:S(2)}) async-start(f32[8,32,2048]{2,1,0:T(8,128)} %stack.5), calls=%async_computation.1 | async-start | bytes 4194304 | tf_op jit(solution)/shard_map/all_to_all | solution.py:20
  30.8 0.0 reduce-scatter.2.cloned.1.call-start
  30.8 0.0 copy-done.2
  30.8 0.1 reshape.18
  31.0 0.1 eq.12
  31.1 26.0 %all-to-all-done.1 = f32[8,32,2048]{2,1,0:T(8,128)S(1)} async-done(((f32[8,32,2048]{2,1,0:T(8,128)}), f32[8,32,2048]{2,1,0:T(8,128)S(1)}, u32[]{:S(2)}, u32[]{:S(2)}) %all-to-all-start.1) | async-done | bytes 2097184 | tf_op jit(solution)/shard_map/all_to_all | solution.py:20
  57.1 1.2 copy.13
  58.4 3.0 %copy.14 = f32[16,8,2,2048]{3,2,1,0:T(2,128)} copy(f32[16,8,2,2048]{3,1,2,0:T(8,128)S(1)} %bitcast.10) | data formatting | bytes 4194304 | tf_op jit(solution)/shard_map/transpose | solution.py:29
  61.3 0.0 copy-start
  61.3 0.0 copy-start.1
  61.3 2.7 %reshape.19 = f32[256,2048]{1,0:T(8,128)S(1)} reshape(f32[16,8,2,2048]{3,2,1,0:T(2,128)} %copy.14) | data formatting | bytes 4194304 | tf_op jit(solution)/shard_map/reshape | solution.py:30
  64.1 0.0 copy-done
  64.1 0.0 copy-done.1
  64.1 18.1 %convolution_select_fusion = f32[256,2048]{1,0:T(8,128)} fusion(f32[2048,2048]{1,0:T(8,128)} %param.6, f32[256,2048]{1,0:T(8,128)S(1)} %reshape.19, s32[2048]{0:T(1024)S(1)} %copy-done, s32[2048]{0:T(1024)S(1)} %copy-done.1, s32[256]{0:T(256)S(1)} %eq.12), kind=kOutput, calls=%fused_computation | convolution fusion | flops 12886999040 | bytes 20988928 | tf_op jit(solution)/shard_map/dot_general | solution.py:8
  82.2 0.0 reduce-scatter.2.cloned.1.call-update
  82.2 69.4 %reduce-scatter.2.cloned.1.call-done = f32[16,2048]{1,0:T(8,128)} async-done(((f32[256,2048]{1,0:T(8,128)}), f32[16,2048]{1,0:T(8,128)}) %reduce-scatter.2.cloned.1.call-update) | async-done | bytes 131088 | tf_op jit(solution)/shard_map/reduce_scatter | solution.py:37
  151.7 1.0 all_to_all.33
  152.7 11.6 %all_to_all.41 = f32[8,2,2048]{2,1,0:T(2,128)S(1)} all-to-all(f32[8,2,2048]{2,1,0:T(2,128)S(1)} %all_to_all.33), channel_id=1, replica_groups=mesh['row'=8,'col'=16] {'row'}, dimensions={0} | all-to-all | bytes 262144 | tf_op jit(solution)/shard_map/all_to_all | solution.py:43
  164.3 0.7 copy.17
  (1 shorter events, 0.0 us)
Async XLA Ops:
  24.4 6.4 %copy-start.2 = (s32[256]{0:T(256)S(1)}, s32[256]{0:T(256)}, u32[]{:S(2)}) copy-start(s32[256]{0:T(256)} %param.7) | copy-start | bytes 3076
  24.4 32.8 %all-to-all-start.1 = ((f32[8,32,2048]{2,1,0:T(8,128)}), f32[8,32,2048]{2,1,0:T(8,128)S(1)}, u32[]{:S(2)}, u32[]{:S(2)}) async-start(f32[8,32,2048]{2,1,0:T(8,128)} %stack.5), calls=%async_computation.1 | async-start | bytes 4194304 | tf_op jit(solution)/shard_map/all_to_all | solution.py:20
  30.8 120.9 %reduce-scatter.2.cloned.1.call-start = ((), (), s32[]{:S(2)}) async-start(), calls=%async_computation.4 | async-start | bytes 2228224 | tf_op jit(solution)/shard_map/reduce_scatter | solution.py:37
  61.3 2.7 %copy-start = (s32[2048]{0:T(1024)S(1)}, s32[2048]{0:T(1024)}, u32[]{:S(2)}) copy-start(s32[2048]{0:T(1024)} %param.9) | copy-start | bytes 24580
  61.3 2.7 %copy-start.1 = (s32[2048]{0:T(1024)S(1)}, s32[2048]{0:T(1024)}, u32[]{:S(2)}) copy-start(s32[2048]{0:T(1024)} %param.8) | copy-start | bytes 24580
Sparse Core Ops, SparseCore 0:
  82.4 69.2 reduce-scatter.1
